TPU v7x, 32 devices: a whole 2x2x4 slice. The times are simulated.
32 devices in a mesh: seq: 8 (over z, y), ep: 4 (over x, core).
Axes of the slice: x: 2, y: 2, z: 4, core: 2. Of those that a mesh axis runs over, the one named last changes fastest.
Arguments:
- queries: bfloat16 [3072, 6144], P('seq', 'ep'), may hold values from -5 to 5
- key_heads: bfloat16 [3072, 1024], P('seq', 'ep'), may hold values from -4 to 4, as said below
- value_heads: bfloat16 [3072, 1024], P('seq', 'ep'), may hold values from -6 to 6, as said below
- attn_grad: bfloat16 [3072, 6144], P('seq', 'ep'), may hold values from -6 to 6
- segments: int32 [3072], P('seq'), may hold values from 0 to 15, never falling along the last dimension, each value on 1 to 1153 neighbouring positions
- moe_grad: bfloat16 [3072, 6144], P(('seq', 'ep')), may hold values from -6 to 6
- expert_out: bfloat16 [3072, 2, 6144], P(('seq', 'ep')), may hold values from -6 to 6
- normed: bfloat16 [3072, 6144], P(('seq', 'ep')), may hold values from -6 to 6
- router: bfloat16 [8, 6144], replicated, may hold values from -0.078125 to 0.078125
- routes: int32 [3072, 2], P(('seq', 'ep')), may hold values from 0 to 7, all different within a row; in each aligned block of 96 rows (0 to 95, 96 to 191, ...) at most 24 rows name the same one
Outputs:
- query_grad: bfloat16 [3072, 6144], P('seq', 'ep')
- key_grad: bfloat16 [3072, 1024], P('seq', 'ep')
- value_grad: bfloat16 [3072, 1024], P('seq', 'ep')
- normed_grad: bfloat16 [3072, 6144], P(('seq', 'ep'))
- router_grad: float32 [8, 6144], replicated
- routed_grads: bfloat16 [128, 48, 6144], P(('seq', 'ep'))
Inputs may be any that keep to these rules, and one draw needn't show every extreme that they name: `key_heads`: the 1 indices of ep e with the same e // 1 hold identical copies. `value_heads`: the 1 indices of ep e with the same e // 1 hold identical copies. `segments`: segment numbers never fall along the sequence; every document has 1 to 1153 tokens and one has exactly 1153. A token names two different experts; in each aligned block of 96 tokens (the tokens of one device) every expert is named by exactly 24 routes.
All inputs are finite; a program needn't handle non-finite values.
Results may differ from a plain program's by a relative error of at most 0.0071.
Values may be sent and summed in bfloat16 or wider, within the bound.
A program may use at most 192 MiB of HBM per device.

v0:
```python
import functools
import math

import jax
import jax.numpy as jnp
from jax import lax
from jax.experimental import pallas as pl
from jax.experimental.pallas import tpu as pltpu
from jax.sharding import PartitionSpec as P

EXPERTS = 8
HD = 128
TOP = 2
REACH = 3
QT = 128
MASKED = -1e30
F32 = jnp.float32
BF16 = jnp.bfloat16
VMEM_LIMIT = 48 * 1024 * 1024
SCALE = 1.0 / math.sqrt(HD)
SCALE2 = SCALE * math.log2(math.e)


def from_behind(value, axis, by):
    devices = lax.axis_size(axis)
    pairs = [(i, i + by) for i in range(devices) if 0 <= i + by < devices]
    return lax.ppermute(value, axis, pairs)


def nt(a, b):
    return lax.dot_general(a, b, (((1,), (1,)), ((), ())), preferred_element_type=F32)


def nn(a, b):
    return jnp.dot(a, b, preferred_element_type=F32)


def attn_kernel(group, tok, aliased, *refs):
    if aliased:
        refs = refs[1:]
    (start_ref, q_ref, g_ref, k0, v0, k1, v1, k2, v2, k3, v3,
     dq_ref, own_ref, far_ref, kcat, vcat, kt, bias, dk, dv) = refs
    step = pl.program_id(0)
    steps = pl.num_programs(0)
    window = REACH * tok + QT

    @pl.when(step == 0)
    def _():
        for n, (k, v) in enumerate(((k3, v3), (k2, v2), (k1, v1), (k0, v0))):
            kcat[n * tok:(n + 1) * tok, :] = k[...]
            vcat[n * tok:(n + 1) * tok, :] = v[...]
            kt[:, n * tok:(n + 1) * tok] = k[...].astype(F32).T.astype(BF16)
        dk[...] = jnp.zeros_like(dk)
        dv[...] = jnp.zeros_like(dv)

    base = pl.multiple_of(step * QT, QT)
    keys = pl.ds(base, window)
    position = lax.broadcasted_iota(jnp.int32, (window, QT), 0)
    limit = REACH * tok + lax.broadcasted_iota(jnp.int32, (window, QT), 1)
    allowed = (position >= start_ref[...] - base) & (position <= limit)
    bias[...] = jnp.where(allowed, 0.0, MASKED)
    together = 2 if group % 2 == 0 else 1
    for first in range(0, group, together):
        heads = range(first, first + together)
        q = jnp.concatenate([q_ref[:, h * HD:(h + 1) * HD] for h in heads], axis=0)
        g = jnp.concatenate([g_ref[:, h * HD:(h + 1) * HD] for h in heads], axis=0)
        kwin = kcat[keys, :]
        scores = nt(kwin, q) + jnp.concatenate([bias[...]] * together, axis=1)
        prob_grad = nt(vcat[keys, :], g)
        peak = jnp.max(scores, axis=0, keepdims=True)
        weights = jnp.exp2((scores - peak) * SCALE2)
        inverse = 1.0 / jnp.sum(weights, axis=0, keepdims=True)
        delta = jnp.sum(weights * prob_grad, axis=0, keepdims=True) * inverse
        probs = weights * inverse
        score_low = (probs * (prob_grad - delta)).astype(BF16)
        dv[keys, :] += nn(probs.astype(BF16), g)
        dk[keys, :] += nn(score_low, q)
        dq = (nn(kt[:, keys], score_low) * SCALE).T.astype(BF16)
        for n, h in enumerate(heads):
            dq_ref[:, h * HD:(h + 1) * HD] = dq[n * QT:(n + 1) * QT, :]

    @pl.when(step == steps - 1)
    def _():
        own_ref[:, :HD] = dk[REACH * tok:, :] * SCALE
        own_ref[:, HD:] = dv[REACH * tok:, :]
        for n in range(REACH):
            rows = slice((REACH - 1 - n) * tok, (REACH - n) * tok)
            far_ref[n, :, :HD] = (dk[rows, :] * SCALE).astype(BF16)
            far_ref[n, :, HD:] = dv[rows, :].astype(BF16)


def attention_head(head, kv_heads, group, start, queries, attn_grad, key_heads, value_heads, far, dq_prev):
    tok = queries.shape[0]
    keys = (REACH + 1) * tok
    width = group * HD
    row_spec = pl.BlockSpec((QT, width), lambda i: (i, head))
    own_spec = pl.BlockSpec((tok, HD), lambda i: (0, head))
    far_k = pl.BlockSpec((tok, HD), lambda i: (0, head))
    far_v = pl.BlockSpec((tok, HD), lambda i: (0, kv_heads + head))
    in_specs = [pl.BlockSpec((1, QT), lambda i: (0, i)), row_spec, row_spec, own_spec, own_spec]
    args = [start, queries, attn_grad, key_heads, value_heads]
    for block in far:
        in_specs += [far_k, far_v]
        args += [block, block]
    aliases = {}
    if dq_prev is not None:
        in_specs = [pl.BlockSpec(memory_space=pl.ANY)] + in_specs
        args = [dq_prev] + args
        aliases = {0: 0}
    work = (tok // QT) * (REACH * tok + QT) * QT * group
    return pl.pallas_call(
        functools.partial(attn_kernel, group, tok, dq_prev is not None),
        grid=(tok // QT,),
        in_specs=in_specs,
        out_specs=(
            row_spec,
            pl.BlockSpec((tok, 2 * HD), lambda i: (0, 0)),
            pl.BlockSpec((REACH, tok, 2 * HD), lambda i: (0, 0, 0)),
        ),
        out_shape=(
            jax.ShapeDtypeStruct(queries.shape, BF16),
            jax.ShapeDtypeStruct((tok, 2 * HD), F32),
            jax.ShapeDtypeStruct((REACH, tok, 2 * HD), BF16),
        ),
        scratch_shapes=[
            pltpu.VMEM((keys, HD), BF16),
            pltpu.VMEM((keys, HD), BF16),
            pltpu.VMEM((HD, keys), BF16),
            pltpu.VMEM((REACH * tok + QT, QT), F32),
            pltpu.VMEM((keys, HD), F32),
            pltpu.VMEM((keys, HD), F32),
        ],
        input_output_aliases=aliases,
        compiler_params=pltpu.CompilerParams(vmem_limit_bytes=VMEM_LIMIT),
        cost_estimate=pl.CostEstimate(flops=work * HD * 10, bytes_accessed=tok * width * 6, transcendentals=work),
        name="attention",
    )(*args)


def split3(x):
    high = x.astype(BF16)
    rest = x - high.astype(F32)
    mid = rest.astype(BF16)
    low = (rest - mid.astype(F32)).astype(BF16)
    return jnp.concatenate([high.astype(F32), mid.astype(F32), low.astype(F32)], axis=0).astype(BF16)


def route_kernel(capacity, copies, all_tokens, routes_ref, moe_ref, expert_ref, normed_ref, router_ref,
                 ngrad_ref, rgrad_ref, out_ref):
    rows, width = moe_ref.shape
    slots = out_ref.shape[0]
    logits = nt(router_ref[...], normed_ref[...])
    expert = lax.broadcasted_iota(jnp.int32, (EXPERTS, rows), 0)
    e0 = routes_ref[0:1, :]
    e1 = routes_ref[1:2, :]
    hot0 = (expert == e0).astype(F32)
    hot1 = (expert == e1).astype(F32)
    chosen0 = jnp.sum(hot0 * logits, axis=0, keepdims=True)
    chosen1 = jnp.sum(hot1 * logits, axis=0, keepdims=True)
    first = 1.0 / (1.0 + jnp.exp(chosen1 - chosen0))
    second = 1.0 - first
    product = nt(expert_ref[...], moe_ref[...])
    which = lax.broadcasted_iota(jnp.int32, product.shape, 0)
    token = lax.broadcasted_iota(jnp.int32, product.shape, 1)
    signed = jnp.where(which == 2 * token, product, jnp.where(which == 2 * token + 1, -product, 0.0))
    step = first * second * jnp.sum(signed, axis=0, keepdims=True)
    pieces = split3((hot0 - hot1) * step)
    earlier = lax.broadcasted_iota(jnp.int32, (rows, rows), 0) < lax.broadcasted_iota(jnp.int32, (rows, rows), 1)
    rank = nn((hot0 + hot1).astype(BF16), earlier.astype(BF16))
    rank0 = jnp.sum(hot0 * rank, axis=0, keepdims=True).astype(jnp.int32)
    rank1 = jnp.sum(hot1 * rank, axis=0, keepdims=True).astype(jnp.int32)
    slot = lax.broadcasted_iota(jnp.int32, (slots, rows), 0)
    slot = (slot // (copies * capacity)) * capacity + slot % capacity
    take0 = slot == e0 * capacity + rank0
    take1 = slot == e1 * capacity + rank1
    gate = jnp.sum(jnp.where(take0, first, 0.0) + jnp.where(take1, second, 0.0), axis=1, keepdims=True)
    pick = (take0 | take1).astype(BF16)
    chunk = 512
    for at in range(0, width, chunk):
        columns = slice(at, at + chunk)
        out_ref[:, columns] = (nn(pick, moe_ref[:, columns]) * gate).astype(BF16)
        table = jnp.concatenate([router_ref[:, columns].astype(F32)] * 3, axis=0).astype(BF16)
        ngrad_ref[:, columns] = lax.dot_general(
            pieces, table, (((0,), (0,)), ((), ())), preferred_element_type=F32
        ).astype(BF16)
        sums = nn(pieces, normed_ref[:, columns])
        rgrad_ref[:, columns] = (
            sums[0:EXPERTS] + sums[EXPERTS:2 * EXPERTS] + sums[2 * EXPERTS:]
        ) * (1.0 / all_tokens)


def on_device(queries, key_heads, value_heads, attn_grad, segments, moe_grad, expert_out, normed, router, routes):
    tok = queries.shape[0]
    kv_heads = key_heads.shape[1] // HD
    group = queries.shape[1] // (kv_heads * HD)
    seq_index = lax.axis_index("seq")
    ep_size = lax.axis_size("ep")
    both = jnp.concatenate([key_heads, value_heads], axis=1)
    far = [from_behind(both, "seq", offset) for offset in range(1, REACH + 1)]
    behind = jnp.int32(0)
    for offset in range(1, REACH + 1):
        segs = from_behind(segments, "seq", offset)
        behind += jnp.where(seq_index >= offset, jnp.sum((segs == segments[0]).astype(jnp.int32)), 0)
    inside = jnp.sum((segments[:, None] < segments[None, :]).astype(jnp.int32), axis=0)
    start = (REACH * tok + inside - jnp.where(segments == segments[0], behind, 0))[None, :]

    moe_rows, width = moe_grad.shape
    capacity = moe_rows * TOP // EXPERTS
    copies = max(1, ep_size // EXPERTS)
    per_device = max(1, EXPERTS // ep_size)
    slots = EXPERTS * copies * capacity
    devices = lax.axis_size("seq") * ep_size
    normed_grad, local_router, outgoing = pl.pallas_call(
        functools.partial(route_kernel, capacity, copies, moe_rows * devices),
        out_shape=(
            jax.ShapeDtypeStruct((moe_rows, width), BF16),
            jax.ShapeDtypeStruct((EXPERTS, width), F32),
            jax.ShapeDtypeStruct((slots, width), BF16),
        ),
        compiler_params=pltpu.CompilerParams(vmem_limit_bytes=VMEM_LIMIT),
        cost_estimate=pl.CostEstimate(flops=8 * slots * moe_rows * width, bytes_accessed=12 * moe_rows * width, transcendentals=0),
        name="routing",
    )(routes.T, moe_grad, expert_out.reshape(TOP * moe_rows, width), normed, router)
    routed_grads = lax.all_to_all(
        outgoing.reshape(ep_size, per_device * capacity, width), "ep", split_axis=0, concat_axis=0, tiled=True
    )
    parts = lax.all_to_all(
        local_router.reshape(devices, -1), ("seq", "ep"), split_axis=0, concat_axis=0, tiled=True
    )
    total = jnp.broadcast_to(jnp.sum(parts, axis=0, keepdims=True), parts.shape)
    router_grad = lax.all_to_all(
        total, ("seq", "ep"), split_axis=0, concat_axis=0, tiled=True
    ).reshape(EXPERTS, width)

    query_grad = None
    key_parts = []
    value_parts = []
    for head in range(kv_heads):
        query_grad, own, away = attention_head(
            head, kv_heads, group, start, queries, attn_grad, key_heads, value_heads, far, query_grad
        )
        for offset in range(1, REACH + 1):
            own = own + from_behind(away[offset - 1], "seq", -offset).astype(F32)
        key_parts.append(own[:, :HD].astype(BF16))
        value_parts.append(own[:, HD:].astype(BF16))
    key_grad = jnp.concatenate(key_parts, axis=1)
    value_grad = jnp.concatenate(value_parts, axis=1)
    return (query_grad, key_grad, value_grad, normed_grad, router_grad, routed_grads)


def solution(mesh):
    return jax.shard_map(
        on_device,
        mesh=mesh,
        in_specs=(
            P("seq", "ep"),
            P("seq", "ep"),
            P("seq", "ep"),
            P("seq", "ep"),
            P("seq"),
            P(("seq", "ep"), None),
            P(("seq", "ep"), None, None),
            P(("seq", "ep"), None),
            P(),
            P(("seq", "ep"), None),
        ),
        out_specs=(
            P("seq", "ep"),
            P("seq", "ep"),
            P("seq", "ep"),
            P(("seq", "ep"), None),
            P(),
            P(("seq", "ep"), None, None),
        ),
        check_vma=False,
    )
```

profile of v0, /device:TPU:10, one launch (start us, length us, event | category | flops | bytes accessed | tf_op | source)
XLA Modules:
  0.0 138.5 jit_solution(6134760223579246380)
XLA Ops:
  0.6 3.4 %collective-permute-start = (s32[384]{0:T(512)}, s32[384]{0:T(512)S(1)}, u32[]{:S(2)}, u32[]{:S(2)}) collective-permute-start(s32[384]{0:T(512)} %param.14), channel_id=1, source_target_pairs={{0,4},{4,8},{8,12},{12,16},{16,20},{20,24},{24,28},{1,5},{5,9},{9,... | collective-permute-start | bytes 4616 | tf_op jit(solution)/shard_map/ppermute | solution.py:27
  4.1 4.4 %collective-permute-start.2 = (s32[384]{0:T(512)}, s32[384]{0:T(512)S(1)}, u32[]{:S(2)}, u32[]{:S(2)}) collective-permute-start(s32[384]{0:T(512)} %param.14), channel_id=1, source_target_pairs={{0,12},{4,16},{8,20},{12,24},{16,28},{1,13},{5,17},{9,21},{13,25},... | collective-permute-start | bytes 4616 | tf_op jit(solution)/shard_map/ppermute | solution.py:27
  8.5 1.9 %collective-permute-start.1 = (s32[384]{0:T(512)}, s32[384]{0:T(512)S(1)}, u32[]{:S(2)}, u32[]{:S(2)}) collective-permute-start(s32[384]{0:T(512)} %param.14), channel_id=1, source_target_pairs={{0,8},{4,12},{8,16},{12,20},{16,24},{20,28},{1,9},{5,13},{9,17},{1... | collective-permute-start | bytes 4616 | tf_op jit(solution)/shard_map/ppermute | solution.py:27
  10.4 1.6 %constant_dynamic-update-slice_fusion.1 = bf16[384,512]{1,0:T(8,128)(2,1)} fusion(bf16[384,256]{1,0:T(8,128)(2,1)} %refs_4_.3), kind=kLoop, calls=%fused_computation.12 | loop fusion | bytes 393216
  12.1 1.6 %constant_dynamic-update-slice_fusion = bf16[384,512]{1,0:T(8,128)(2,1)} fusion(bf16[384,512]{1,0:T(8,128)(2,1)} %constant_dynamic-update-slice_fusion.1, bf16[384,256]{1,0:T(8,128)(2,1)} %refs_5_.1), kind=kLoop, calls=%fused_computation.11 | loop fusion | bytes 393216 | tf_op jit(solution)/shard_map/concatenate | solution.py:198
  13.7 1.4 %collective-permute-start.5 = (bf16[384,512]{1,0:T(8,128)(2,1)}, bf16[384,512]{1,0:T(8,128)(2,1)S(1)}, u32[]{:S(2)}, u32[]{:S(2)}) collective-permute-start(bf16[384,512]{1,0:T(8,128)(2,1)} %constant_dynamic-update-slice_fusion), channel_id=1, source_target_pairs={{0,12},{4,16},{8,20},{12,24},{16,28},{1,13},{5,17},{9,21},{13,25},... | collective-permute-start | bytes 1179656 | tf_op jit(solution)/shard_map/ppermute | solution.py:27
  15.1 2.5 %collective-permute-start.4 = (bf16[384,512]{1,0:T(8,128)(2,1)}, bf16[384,512]{1,0:T(8,128)(2,1)S(1)}, u32[]{:S(2)}, u32[]{:S(2)}) collective-permute-start(bf16[384,512]{1,0:T(8,128)(2,1)} %constant_dynamic-update-slice_fusion), channel_id=1, source_target_pairs={{0,8},{4,12},{8,16},{12,20},{16,24},{20,28},{1,9},{5,13},{9,17},{1... | collective-permute-start | bytes 1179656 | tf_op jit(solution)/shard_map/ppermute | solution.py:27
  17.7 4.2 %reshape.34.expert_ref = bf16[192,6144]{1,0:T(8,128)(2,1)} reshape(bf16[96,2,6144]{2,1,0:T(2,128)(2,1)} %param.16) | data formatting | bytes 4718592 | tf_op jit(solution)/shard_map/reshape | solution.py:223
  21.9 6.3 %routing.1 = (bf16[96,6144]{1,0:T(8,128)(2,1)}, f32[8,6144]{1,0:T(8,128)S(1)}, bf16[192,6144]{1,0:T(8,128)(2,1)}) custom-call(s32[2,96]{1,0:T(2,128)S(1)} %bitcast.15, bf16[96,6144]{1,0:T(8,128)(2,1)S(1)} %copy-done, bf16[192,6144]{1,0:T(8,128)(2,1)} %reshape.34.expert_ref, bf16[96,6144]{1,0:T(8,128)(2,1)S(1)} %copy-done.1, bf16[8,6144]{1,0:T(8,128)(2,1)S(1)} %copy-done.4), custom_call_target="tpu_custom_call" | custom-call | flops 905969664 | bytes 7077888 | tf_op jit(solution)/shard_map/routing/pallas_call | solution.py:213
  29.2 4.6 %all-to-all-start = ((f32[32,1,1536]{2,1,0:T(1,128)}), f32[32,1,1536]{2,1,0:T(1,128)S(1)}, u32[]{:S(2)}, u32[]{:S(2)}) async-start(f32[32,1,1536]{2,1,0:T(1,128)} %all_to_all.17), calls=%async_computation | async-start | bytes 393216 | tf_op jit(solution)/shard_map/all_to_all | solution.py:227
  34.5 3.4 %collective-permute-start.3 = (bf16[384,512]{1,0:T(8,128)(2,1)}, bf16[384,512]{1,0:T(8,128)(2,1)S(1)}, u32[]{:S(2)}, u32[]{:S(2)}) collective-permute-start(bf16[384,512]{1,0:T(8,128)(2,1)} %constant_dynamic-update-slice_fusion), channel_id=1, source_target_pairs={{0,4},{4,8},{8,12},{12,16},{16,20},{20,24},{24,28},{1,5},{5,9},{9,... | collective-permute-start | bytes 1179656 | tf_op jit(solution)/shard_map/ppermute | solution.py:27
  37.9 1.3 convert_reduce_fusion.3
  39.2 1.3 convert_reduce_fusion.1
  41.7 1.3 convert_reduce_fusion.2
  44.6 8.9 %all-to-all-start.1 = ((f32[32,1,1536]{2,1,0:T(1,128)}), f32[32,1,1536]{2,1,0:T(1,128)S(1)}, u32[]{:S(2)}, u32[]{:S(2)}) async-start(f32[32,1,1536]{2,1,0:T(1,128)} %broadcast_in_dim.22), calls=%async_computation.1 | async-start | bytes 393216 | tf_op jit(solution)/shard_map/all_to_all | solution.py:231
  54.3 1.3 copy-done.6
  55.5 1.3 copy-done.8
  56.8 14.3 %attention.2 = (bf16[384,1536]{1,0:T(8,128)(2,1)}, f32[384,256]{1,0:T(8,128)S(1)}, bf16[3,384,256]{2,1,0:T(8,128)(2,1)S(1)}) custom-call(s32[1,384]{1,0:T(1,128)S(1)} %broadcast_in_dim.21.refs_0_.refs_1_, bf16[384,1536]{1,0:T(8,128)(2,1)S(1)} %copy-done.6, bf16[384,1536]{1,0:T(8,128)(2,1)S(1)} %copy-done.8, bf16[384,256]{1,0:T(8,128)(2,1)S(1)} %copy-done.2, ...), custom_call_target="tpu_custom_call" | custom-call | flops 3774873600 | bytes 1769472 | tf_op jit(solution)/shard_map/attention/pallas_call | solution.py:111
  71.8 5.2 %all-to-all-start.2 = ((bf16[4,48,6144]{2,1,0:T(8,128)(2,1)}), bf16[4,48,6144]{2,1,0:T(8,128)(2,1)}, u32[]{:S(2)}, u32[]{:S(2)}) async-start(bf16[4,48,6144]{2,1,0:T(8,128)(2,1)} %bitcast.8), calls=%async_computation.2 | async-start | bytes 4718592 | tf_op jit(solution)/shard_map/all_to_all | solution.py:224
  77.0 1.3 copy-done.9
  78.3 1.0 copy-done.11
  79.2 14.3 %attention.3 = (bf16[384,1536]{1,0:T(8,128)(2,1)}, f32[384,256]{1,0:T(8,128)S(1)}, bf16[3,384,256]{2,1,0:T(8,128)(2,1)S(1)}) custom-call(bf16[384,1536]{1,0:T(8,128)(2,1)} %get-tuple-element.15.refs_0_, s32[1,384]{1,0:T(1,128)S(1)} %broadcast_in_dim.21.refs_0_.refs_1_, bf16[384,1536]{1,0:T(8,128)(2,1)S(1)} %copy-done.7, ...), custom_call_target="tpu_custom_call", output_to_operand_aliasing={{0}: (0, {})} | custom-call | flops 3774873600 | bytes 1769472 | tf_op jit(solution)/shard_map/attention/pallas_call | solution.py:111
  93.6 3.4 %collective-permute-start.9 = (bf16[384,256]{1,0:T(8,128)(2,1)S(1)}, bf16[384,256]{1,0:T(8,128)(2,1)S(1)}, u32[]{:S(2)}, u32[]{:S(2)}) collective-permute-start(bf16[384,256]{1,0:T(8,128)(2,1)S(1)} %get-tuple-element.27), channel_id=1, source_target_pairs={{4,0},{8,4},{12,8},{16,12},{20,16},{24,20},{28,24},{5,1},{9,5},{13... | collective-permute-start | bytes 589832 | tf_op jit(solution)/shard_map/ppermute | solution.py:27
  97.0 1.3 collective-permute-start.11
  98.3 1.9 %collective-permute-start.10 = (bf16[384,256]{1,0:T(8,128)(2,1)S(1)}, bf16[384,256]{1,0:T(8,128)(2,1)S(1)}, u32[]{:S(2)}, u32[]{:S(2)}) collective-permute-start(bf16[384,256]{1,0:T(8,128)(2,1)S(1)} %get-tuple-element.29), channel_id=1, source_target_pairs={{8,0},{12,4},{16,8},{20,12},{24,16},{28,20},{9,1},{13,5},{17,9},{2... | collective-permute-start | bytes 589832 | tf_op jit(solution)/shard_map/ppermute | solution.py:27
  100.3 1.9 %collective-permute-start.6 = (bf16[384,256]{1,0:T(8,128)(2,1)S(1)}, bf16[384,256]{1,0:T(8,128)(2,1)S(1)}, u32[]{:S(2)}, u32[]{:S(2)}) collective-permute-start(bf16[384,256]{1,0:T(8,128)(2,1)S(1)} %get-tuple-element.24), channel_id=1, source_target_pairs={{4,0},{8,4},{12,8},{16,12},{20,16},{24,20},{28,24},{5,1},{9,5},{13... | collective-permute-start | bytes 589832 | tf_op jit(solution)/shard_map/ppermute | solution.py:27
  102.2 1.3 collective-permute-start.8
  103.5 2.4 %collective-permute-done.9 = bf16[384,256]{1,0:T(8,128)(2,1)S(1)} collective-permute-done((bf16[384,256]{1,0:T(8,128)(2,1)S(1)}, bf16[384,256]{1,0:T(8,128)(2,1)S(1)}, u32[]{:S(2)}, u32[]{:S(2)}) %collective-permute-start.9) | collective-permute-done | bytes 196640 | tf_op jit(solution)/shard_map/ppermute | solution.py:27
  105.9 3.7 %collective-permute-start.7 = (bf16[384,256]{1,0:T(8,128)(2,1)S(1)}, bf16[384,256]{1,0:T(8,128)(2,1)S(1)}, u32[]{:S(2)}, u32[]{:S(2)}) collective-permute-start(bf16[384,256]{1,0:T(8,128)(2,1)S(1)} %get-tuple-element.26), channel_id=1, source_target_pairs={{8,0},{12,4},{16,8},{20,12},{24,16},{28,20},{9,1},{13,5},{17,9},{2... | collective-permute-start | bytes 589832 | tf_op jit(solution)/shard_map/ppermute | solution.py:27
  109.6 7.8 %collective-permute-done.10 = bf16[384,256]{1,0:T(8,128)(2,1)S(1)} collective-permute-done((bf16[384,256]{1,0:T(8,128)(2,1)S(1)}, bf16[384,256]{1,0:T(8,128)(2,1)S(1)}, u32[]{:S(2)}, u32[]{:S(2)}) %collective-permute-start.10) | collective-permute-done | bytes 196640 | tf_op jit(solution)/shard_map/ppermute | solution.py:27
  117.6 15.4 %collective-permute-done.7 = bf16[384,256]{1,0:T(8,128)(2,1)S(1)} collective-permute-done((bf16[384,256]{1,0:T(8,128)(2,1)S(1)}, bf16[384,256]{1,0:T(8,128)(2,1)S(1)}, u32[]{:S(2)}, u32[]{:S(2)}) %collective-permute-start.7) | collective-permute-done | bytes 196640 | tf_op jit(solution)/shard_map/ppermute | solution.py:27
  135.2 3.3 %copy.22 = bf16[4,48,6144]{2,1,0:T(8,128)(2,1)} copy(bf16[4,48,6144]{2,1,0:T(8,128)(2,1)} %all-to-all-done.2) | data formatting | bytes 4718592
  (54 shorter events, 6.2 us)
Async XLA Ops:
  0.6 33.8 %collective-permute-start = (s32[384]{0:T(512)}, s32[384]{0:T(512)S(1)}, u32[]{:S(2)}, u32[]{:S(2)}) collective-permute-start(s32[384]{0:T(512)} %param.14), channel_id=1, source_target_pairs={{0,4},{4,8},{8,12},{12,16},{16,20},{20,24},{24,28},{1,5},{5,9},{9,... | collective-permute-start | bytes 4616 | tf_op jit(solution)/shard_map/ppermute | solution.py:27
  4.1 35.1 %collective-permute-start.2 = (s32[384]{0:T(512)}, s32[384]{0:T(512)S(1)}, u32[]{:S(2)}, u32[]{:S(2)}) collective-permute-start(s32[384]{0:T(512)} %param.14), channel_id=1, source_target_pairs={{0,12},{4,16},{8,20},{12,24},{16,28},{1,13},{5,17},{9,21},{13,25},... | collective-permute-start | bytes 4616 | tf_op jit(solution)/shard_map/ppermute | solution.py:27
  8.5 33.2 %collective-permute-start.1 = (s32[384]{0:T(512)}, s32[384]{0:T(512)S(1)}, u32[]{:S(2)}, u32[]{:S(2)}) collective-permute-start(s32[384]{0:T(512)} %param.14), channel_id=1, source_target_pairs={{0,8},{4,12},{8,16},{12,20},{16,24},{20,28},{1,9},{5,13},{9,17},{1... | collective-permute-start | bytes 4616 | tf_op jit(solution)/shard_map/ppermute | solution.py:27
  13.7 8.2 %copy-start = (bf16[96,6144]{1,0:T(8,128)(2,1)S(1)}, bf16[96,6144]{1,0:T(8,128)(2,1)}, u32[]{:S(2)}) copy-start(bf16[96,6144]{1,0:T(8,128)(2,1)} %moe_ref.1) | copy-start | bytes 3538948
  13.7 8.2 %copy-start.1 = (bf16[96,6144]{1,0:T(8,128)(2,1)S(1)}, bf16[96,6144]{1,0:T(8,128)(2,1)}, u32[]{:S(2)}) copy-start(bf16[96,6144]{1,0:T(8,128)(2,1)} %normed_ref.1) | copy-start | bytes 3538948
  13.7 8.2 %copy-start.4 = (bf16[8,6144]{1,0:T(8,128)(2,1)S(1)}, bf16[8,6144]{1,0:T(8,128)(2,1)}, u32[]{:S(2)}) copy-start(bf16[8,6144]{1,0:T(8,128)(2,1)} %router_ref.1) | copy-start | bytes 294916
  13.7 8.2 %copy-start.5 = (s32[96,2]{0,1:T(2,128)S(1)}, s32[96,2]{0,1:T(2,128)}, u32[]{:S(2)}) copy-start(s32[96,2]{0,1:T(2,128)} %param.19) | copy-start | bytes 2308
  13.7 40.5 %collective-permute-start.5 = (bf16[384,512]{1,0:T(8,128)(2,1)}, bf16[384,512]{1,0:T(8,128)(2,1)S(1)}, u32[]{:S(2)}, u32[]{:S(2)}) collective-permute-start(bf16[384,512]{1,0:T(8,128)(2,1)} %constant_dynamic-update-slice_fusion), channel_id=1, source_target_pairs={{0,12},{4,16},{8,20},{12,24},{16,28},{1,13},{5,17},{9,21},{13,25},... | collective-permute-start | bytes 1179656 | tf_op jit(solution)/shard_map/ppermute | solution.py:27
  15.1 39.1 %collective-permute-start.4 = (bf16[384,512]{1,0:T(8,128)(2,1)}, bf16[384,512]{1,0:T(8,128)(2,1)S(1)}, u32[]{:S(2)}, u32[]{:S(2)}) collective-permute-start(bf16[384,512]{1,0:T(8,128)(2,1)} %constant_dynamic-update-slice_fusion), channel_id=1, source_target_pairs={{0,8},{4,12},{8,16},{12,20},{16,24},{20,28},{1,9},{5,13},{9,17},{1... | collective-permute-start | bytes 1179656 | tf_op jit(solution)/shard_map/ppermute | solution.py:27
  21.9 11.9 %copy-start.14 = (s32[384]{0:T(512)S(1)}, s32[384]{0:T(512)}, u32[]{:S(2)}) copy-start(s32[384]{0:T(512)} %param.14) | copy-start | bytes 4612
  28.2 26.0 %copy-start.2 = (bf16[384,256]{1,0:T(8,128)(2,1)S(1)}, bf16[384,256]{1,0:T(8,128)(2,1)}, u32[]{:S(2)}) copy-start(bf16[384,256]{1,0:T(8,128)(2,1)} %refs_4_.3) | copy-start | bytes 589828
  28.2 26.0 %copy-start.3 = (bf16[384,256]{1,0:T(8,128)(2,1)S(1)}, bf16[384,256]{1,0:T(8,128)(2,1)}, u32[]{:S(2)}) copy-start(bf16[384,256]{1,0:T(8,128)(2,1)} %refs_5_.1) | copy-start | bytes 589828
  29.2 14.5 %all-to-all-start = ((f32[32,1,1536]{2,1,0:T(1,128)}), f32[32,1,1536]{2,1,0:T(1,128)S(1)}, u32[]{:S(2)}, u32[]{:S(2)}) async-start(f32[32,1,1536]{2,1,0:T(1,128)} %all_to_all.17), calls=%async_computation | async-start | bytes 393216 | tf_op jit(solution)/shard_map/all_to_all | solution.py:227
  34.5 19.7 %collective-permute-start.3 = (bf16[384,512]{1,0:T(8,128)(2,1)}, bf16[384,512]{1,0:T(8,128)(2,1)S(1)}, u32[]{:S(2)}, u32[]{:S(2)}) collective-permute-start(bf16[384,512]{1,0:T(8,128)(2,1)} %constant_dynamic-update-slice_fusion), channel_id=1, source_target_pairs={{0,4},{4,8},{8,12},{12,16},{16,20},{20,24},{24,28},{1,5},{5,9},{9,... | collective-permute-start | bytes 1179656 | tf_op jit(solution)/shard_map/ppermute | solution.py:27
  44.6 26.5 %all-to-all-start.1 = ((f32[32,1,1536]{2,1,0:T(1,128)}), f32[32,1,1536]{2,1,0:T(1,128)S(1)}, u32[]{:S(2)}, u32[]{:S(2)}) async-start(f32[32,1,1536]{2,1,0:T(1,128)} %broadcast_in_dim.22), calls=%async_computation.1 | async-start | bytes 393216 | tf_op jit(solution)/shard_map/all_to_all | solution.py:231
  54.2 1.3 copy-start.6
  55.5 1.3 copy-start.8
  56.8 14.3 %copy-start.10 = (bf16[384,512]{1,0:T(8,128)(2,1)}, bf16[384,512]{1,0:T(8,128)(2,1)S(1)}, u32[]{:S(2)}) copy-start(bf16[384,512]{1,0:T(8,128)(2,1)S(1)} %collective-permute-done.3.refs_5_.refs_6_.refs_7_) | copy-start | bytes 1179652
  71.1 0.7 copy-start.12
  71.8 5.2 %copy-start.7 = (bf16[384,1536]{1,0:T(8,128)(2,1)S(1)}, bf16[384,1536]{1,0:T(8,128)(2,1)}, u32[]{:S(2)}) copy-start(bf16[384,1536]{1,0:T(8,128)(2,1)} %refs_2_.3) | copy-start | bytes 3538948
  71.8 63.4 %all-to-all-start.2 = ((bf16[4,48,6144]{2,1,0:T(8,128)(2,1)}), bf16[4,48,6144]{2,1,0:T(8,128)(2,1)}, u32[]{:S(2)}, u32[]{:S(2)}) async-start(bf16[4,48,6144]{2,1,0:T(8,128)(2,1)} %bitcast.8), calls=%async_computation.2 | async-start | bytes 4718592 | tf_op jit(solution)/shard_map/all_to_all | solution.py:224
  77.0 1.3 copy-start.9
  78.2 1.0 copy-start.11
  93.6 12.3 %collective-permute-start.9 = (bf16[384,256]{1,0:T(8,128)(2,1)S(1)}, bf16[384,256]{1,0:T(8,128)(2,1)S(1)}, u32[]{:S(2)}, u32[]{:S(2)}) collective-permute-start(bf16[384,256]{1,0:T(8,128)(2,1)S(1)} %get-tuple-element.27), channel_id=1, source_target_pairs={{4,0},{8,4},{12,8},{16,12},{20,16},{24,20},{28,24},{5,1},{9,5},{13... | collective-permute-start | bytes 589832 | tf_op jit(solution)/shard_map/ppermute | solution.py:27
  97.0 12.6 %collective-permute-start.11 = (bf16[384,256]{1,0:T(8,128)(2,1)S(1)}, bf16[384,256]{1,0:T(8,128)(2,1)S(1)}, u32[]{:S(2)}, u32[]{:S(2)}) collective-permute-start(bf16[384,256]{1,0:T(8,128)(2,1)S(1)} %get-tuple-element.28), channel_id=1, source_target_pairs={{12,0},{16,4},{20,8},{24,12},{28,16},{13,1},{17,5},{21,9},{25,13},... | collective-permute-start | bytes 589832 | tf_op jit(solution)/shard_map/ppermute | solution.py:27
  98.3 19.2 %collective-permute-start.10 = (bf16[384,256]{1,0:T(8,128)(2,1)S(1)}, bf16[384,256]{1,0:T(8,128)(2,1)S(1)}, u32[]{:S(2)}, u32[]{:S(2)}) collective-permute-start(bf16[384,256]{1,0:T(8,128)(2,1)S(1)} %get-tuple-element.29), channel_id=1, source_target_pairs={{8,0},{12,4},{16,8},{20,12},{24,16},{28,20},{9,1},{13,5},{17,9},{2... | collective-permute-start | bytes 589832 | tf_op jit(solution)/shard_map/ppermute | solution.py:27
  100.3 17.3 %collective-permute-start.6 = (bf16[384,256]{1,0:T(8,128)(2,1)S(1)}, bf16[384,256]{1,0:T(8,128)(2,1)S(1)}, u32[]{:S(2)}, u32[]{:S(2)}) collective-permute-start(bf16[384,256]{1,0:T(8,128)(2,1)S(1)} %get-tuple-element.24), channel_id=1, source_target_pairs={{4,0},{8,4},{12,8},{16,12},{20,16},{24,20},{28,24},{5,1},{9,5},{13... | collective-permute-start | bytes 589832 | tf_op jit(solution)/shard_map/ppermute | solution.py:27
  102.2 15.4 %collective-permute-start.8 = (bf16[384,256]{1,0:T(8,128)(2,1)S(1)}, bf16[384,256]{1,0:T(8,128)(2,1)S(1)}, u32[]{:S(2)}, u32[]{:S(2)}) collective-permute-start(bf16[384,256]{1,0:T(8,128)(2,1)S(1)} %get-tuple-element.25), channel_id=1, source_target_pairs={{12,0},{16,4},{20,8},{24,12},{28,16},{13,1},{17,5},{21,9},{25,13},... | collective-permute-start | bytes 589832 | tf_op jit(solution)/shard_map/ppermute | solution.py:27
  105.9 27.1 %collective-permute-start.7 = (bf16[384,256]{1,0:T(8,128)(2,1)S(1)}, bf16[384,256]{1,0:T(8,128)(2,1)S(1)}, u32[]{:S(2)}, u32[]{:S(2)}) collective-permute-start(bf16[384,256]{1,0:T(8,128)(2,1)S(1)} %get-tuple-element.26), channel_id=1, source_target_pairs={{8,0},{12,4},{16,8},{20,12},{24,16},{28,20},{9,1},{13,5},{17,9},{2... | collective-permute-start | bytes 589832 | tf_op jit(solution)/shard_map/ppermute | solution.py:27
  133.1 0.9 copy-start.13
where the time goes:
time: 140 us; the launch traced here: 139 us
  starting transfers between devices  49.3 us (35%)
  Pallas kernels  35 us (25%)
  waiting for transfers between devices  25.7 us (18%)
  local copies, waits for them, and re-layouts  19.4 us (14%)
  other arithmetic  6.18 us (4%)
  between operations  2.91 us (2%)
    ppermute x12, starting transfers between devices, from_behind(): return lax.ppermute(value, axis, pairs)  30.6 us
    pallas_call x2, Pallas kernels, attention_head(): pl.pallas_call(functools.partial(attn_kernel, group, tok, dq_prev is not...  28.7 us
    ppermute x12, waiting for transfers between devices, from_behind(): return lax.ppermute(value, axis, pairs)  25.7 us
    unnamed x32, local copies, waits for them, and re-layouts  10.4 us
    all_to_all x1, starting transfers between devices, on_device(): lax.all_to_all(total, ('seq', 'ep'), split_axis=0, concat_axis=0, tiled=T...  8.9 us
    pallas_call x1, Pallas kernels, on_device(): pl.pallas_call(functools.partial(route_kernel, capacity, copies, moe_rows...  6.29 us
    all_to_all x1, starting transfers between devices, on_device(): lax.all_to_all(outgoing.reshape(ep_size, per_device * capacity, width), '...  5.16 us
    all_to_all x1, starting transfers between devices, on_device(): lax.all_to_all(local_router.reshape(devices, -1), ('seq', 'ep'), split_ax...  4.63 us
  transfers between devices with their start and end apart: 15, of which 3 were waited for; matrix products, arithmetic and copies ran while one was open for 11% of the time, Pallas kernels for 25%

commit v1 on v0

v1 whole, which is shorter than its diff:
```python
import functools
import math

import jax
import jax.numpy as jnp
from jax import lax
from jax.experimental import pallas as pl
from jax.experimental.pallas import tpu as pltpu
from jax.sharding import PartitionSpec as P

EXPERTS = 8
HD = 128
TOP = 2
REACH = 3
QT = 128
MASKED = -1e30
F32 = jnp.float32
BF16 = jnp.bfloat16
VMEM_LIMIT = 48 * 1024 * 1024
SCALE = 1.0 / math.sqrt(HD)
SCALE2 = SCALE * math.log2(math.e)


def nt(a, b):
    return lax.dot_general(a, b, (((1,), (1,)), ((), ())), preferred_element_type=F32)


def nn(a, b):
    return jnp.dot(a, b, preferred_element_type=F32)


def attn_kernel(group, tok, kv_heads, start_in, seg_ref, q_ref, g_ref, k_ref, v_ref, part_ref,
                dq_ref, dk_ref, dv_ref, total_ref,
                kcat, vcat, kt, bias, dk, dv, start_ref, own, far, back, segs, one, two, two_sum, three, three_sum,
                seg_send, seg_recv, kv_send, kv_recv, far_send, far_recv,
                one_send, one_recv, two_send, two_recv, three_send, three_recv):
    window = REACH * tok + QT
    seq_size = lax.axis_size("seq")
    ep_size = lax.axis_size("ep")
    seq_me = lax.axis_index("seq")
    ep_me = lax.axis_index("ep")
    chunk = part_ref.shape[1] // ep_size

    def seq_at(by):
        return {"seq": lax.rem(seq_me + by + seq_size, seq_size)}

    def ep_at(by):
        return {"ep": lax.rem(ep_me + by, ep_size)}

    def send(src, dst, sent, landed, device):
        return pltpu.make_async_remote_copy(
            src_ref=src, dst_ref=dst, send_sem=sent, recv_sem=landed,
            device_id=device, device_id_type=pl.DeviceIdType.MESH,
        )

    barrier = pltpu.get_barrier_semaphore()
    for by in range(1, seq_size):
        pl.semaphore_signal(barrier, inc=1, device_id=seq_at(by), device_id_type=pl.DeviceIdType.MESH)
    for by in range(1, ep_size):
        pl.semaphore_signal(barrier, inc=1, device_id=ep_at(by), device_id_type=pl.DeviceIdType.MESH)
    pl.semaphore_wait(barrier, seq_size + ep_size - 2)

    seg_copies = []
    for n in range(REACH):
        seg_copies.append(send(seg_ref, segs.at[n], seg_send.at[n], seg_recv.at[n], seq_at(n + 1)))
        seg_copies[-1].start()
    kv_copies = []
    for h in range(kv_heads):
        for n in range(REACH):
            rows = pl.ds((REACH - 1 - n) * tok, tok)
            columns = pl.ds(h * HD, HD)
            for which, (src, dst) in enumerate(((k_ref, kcat), (v_ref, vcat))):
                kv_copies.append(send(
                    src.at[:, columns], dst.at[h, rows, :],
                    kv_send.at[h, n, which], kv_recv.at[h, n, which], seq_at(n + 1),
                ))
        if h == 0:
            for copy in kv_copies:
                copy.start()
            one_copies = []
            for by in range(1, ep_size):
                columns = pl.ds(pl.multiple_of(lax.rem(ep_me + by, ep_size) * chunk, 128), chunk)
                one_copies.append(send(
                    part_ref.at[:, columns], one.at[by - 1], one_send.at[by - 1], one_recv.at[by - 1], ep_at(by)
                ))
                one_copies[-1].start()
        else:
            for copy in kv_copies[-2 * REACH:]:
                copy.start()
    for h in range(kv_heads):
        kcat[h, REACH * tok:, :] = k_ref[:, h * HD:(h + 1) * HD]
        vcat[h, REACH * tok:, :] = v_ref[:, h * HD:(h + 1) * HD]

    for copy in seg_copies:
        copy.wait_recv()
    opening = seg_ref[0:1, 0:1]
    behind = jnp.zeros((1, 1), F32)
    for n in range(REACH):
        same = jnp.where(segs[n, 0:1, :] == opening, 1.0, 0.0)
        count = jnp.sum(same, axis=1, keepdims=True)
        behind += count * jnp.where(seq_me > n, 1.0, 0.0)
    shift = jnp.where(seg_ref[0:1, :] == opening, behind, 0.0)
    start_ref[...] = start_in[...] - shift.astype(jnp.int32)

    mine = pl.ds(pl.multiple_of(ep_me * chunk, 128), chunk)
    partial = part_ref[:, mine]
    for copy in one_copies:
        copy.wait_recv()
    for by in range(1, ep_size):
        partial += one[by - 1]
    two_sum[...] = partial
    two[seq_me] = partial
    two_copies = []
    for by in range(1, seq_size):
        two_copies.append(send(
            two_sum, two.at[seq_me], two_send.at[by - 1], two_recv.at[by - 1], seq_at(by)
        ))
        two_copies[-1].start()

    together = 2 if group % 2 == 0 else 1
    three_copies = []
    far_copies = []
    for h in range(kv_heads):
        for copy in kv_copies[2 * REACH * h:2 * REACH * (h + 1)]:
            copy.wait_recv()
        for n in range(REACH + 1):
            rows = slice(n * tok, (n + 1) * tok)
            kt[:, rows] = kcat[h, rows, :].astype(F32).T.astype(BF16)
        dk[...] = jnp.zeros_like(dk)
        dv[...] = jnp.zeros_like(dv)

        def rows_step(step, carry, h=h):
            base = pl.multiple_of(step * QT, QT)
            keys = pl.ds(base, window)
            rows = pl.ds(base, QT)
            position = lax.broadcasted_iota(jnp.int32, (window, QT), 0)
            limit = REACH * tok + lax.broadcasted_iota(jnp.int32, (window, QT), 1)
            allowed = (position >= start_ref[:, rows] - base) & (position <= limit)
            bias[...] = jnp.where(allowed, 0.0, MASKED)
            for first in range(h * group, (h + 1) * group, together):
                heads = range(first, first + together)
                q = jnp.concatenate([q_ref[rows, i * HD:(i + 1) * HD] for i in heads], axis=0)
                g = jnp.concatenate([g_ref[rows, i * HD:(i + 1) * HD] for i in heads], axis=0)
                scores = nt(kcat[h, keys, :], q) + jnp.concatenate([bias[...]] * together, axis=1)
                prob_grad = nt(vcat[h, keys, :], g)
                peak = jnp.max(scores, axis=0, keepdims=True)
                weights = jnp.exp2((scores - peak) * SCALE2)
                inverse = 1.0 / jnp.sum(weights, axis=0, keepdims=True)
                delta = jnp.sum(weights * prob_grad, axis=0, keepdims=True) * inverse
                probs = weights * inverse
                score_low = (probs * (prob_grad - delta)).astype(BF16)
                dv[keys, :] += nn(probs.astype(BF16), g)
                dk[keys, :] += nn(score_low, q)
                dq = (nn(kt[:, keys], score_low) * SCALE).T.astype(BF16)
                for n, i in enumerate(heads):
                    dq_ref[rows, i * HD:(i + 1) * HD] = dq[n * QT:(n + 1) * QT, :]
            return carry

        lax.fori_loop(0, tok // QT, rows_step, 0)
        for n in range(REACH):
            rows = slice((REACH - 1 - n) * tok, (REACH - n) * tok)
            far[h, n, :, :HD] = (dk[rows, :] * SCALE).astype(BF16)
            far[h, n, :, HD:] = dv[rows, :].astype(BF16)
            copy = send(far.at[h, n], back.at[h, n], far_send.at[h, n], far_recv.at[h, n], seq_at(-(n + 1)))
            copy.start()
            far_copies.append(copy)
        own[h, :, :HD] = dk[REACH * tok:, :] * SCALE
        own[h, :, HD:] = dv[REACH * tok:, :]
        if h == 0:
            for copy in two_copies:
                copy.wait_recv()
            total = two[0]
            for at in range(1, seq_size):
                total += two[at]
            three_sum[...] = total
            three[:, mine] = total
            for by in range(1, ep_size):
                three_copies.append(send(
                    three_sum, three.at[:, mine], three_send.at[by - 1], three_recv.at[by - 1], ep_at(by)
                ))
                three_copies[-1].start()

    for copy in three_copies:
        copy.wait_recv()
    total_ref[...] = three[...]
    for h in range(kv_heads):
        terms = own[h]
        for n in range(REACH):
            far_copies[h * REACH + n].wait_recv()
            terms += back[h, n].astype(F32)
        dk_ref[:, h * HD:(h + 1) * HD] = terms[:, :HD].astype(BF16)
        dv_ref[:, h * HD:(h + 1) * HD] = terms[:, HD:].astype(BF16)
    for copy in seg_copies + kv_copies + one_copies + two_copies + three_copies + far_copies:
        copy.wait_send()


def attention(start, segments, queries, attn_grad, key_heads, value_heads, part):
    tok = queries.shape[0]
    kv_heads = key_heads.shape[1] // HD
    group = queries.shape[1] // (kv_heads * HD)
    keys = (REACH + 1) * tok
    seq_size = lax.axis_size("seq")
    ep_size = lax.axis_size("ep")
    width = part.shape[1]
    chunk = width // ep_size
    work = (tok // QT) * (REACH * tok + QT) * QT * group * kv_heads
    whole = pl.BlockSpec(memory_space=pltpu.VMEM)
    dma = pltpu.SemaphoreType.DMA
    return pl.pallas_call(
        functools.partial(attn_kernel, group, tok, kv_heads),
        in_specs=[whole] * 7,
        out_specs=(whole,) * 4,
        out_shape=(
            jax.ShapeDtypeStruct(queries.shape, BF16),
            jax.ShapeDtypeStruct(key_heads.shape, BF16),
            jax.ShapeDtypeStruct(value_heads.shape, BF16),
            jax.ShapeDtypeStruct(part.shape, F32),
        ),
        scratch_shapes=[
            pltpu.VMEM((kv_heads, keys, HD), BF16),
            pltpu.VMEM((kv_heads, keys, HD), BF16),
            pltpu.VMEM((HD, keys), BF16),
            pltpu.VMEM((REACH * tok + QT, QT), F32),
            pltpu.VMEM((keys, HD), F32),
            pltpu.VMEM((keys, HD), F32),
            pltpu.VMEM((1, tok), jnp.int32),
            pltpu.VMEM((kv_heads, tok, 2 * HD), F32),
            pltpu.VMEM((kv_heads, REACH, tok, 2 * HD), BF16),
            pltpu.VMEM((kv_heads, REACH, tok, 2 * HD), BF16),
            pltpu.VMEM((REACH, 8, tok), jnp.int32),
            pltpu.VMEM((ep_size - 1, EXPERTS, chunk), F32),
            pltpu.VMEM((seq_size, EXPERTS, chunk), F32),
            pltpu.VMEM((EXPERTS, chunk), F32),
            pltpu.VMEM((EXPERTS, width), F32),
            pltpu.VMEM((EXPERTS, chunk), F32),
            dma((REACH,)),
            dma((REACH,)),
            dma((kv_heads, REACH, 2)),
            dma((kv_heads, REACH, 2)),
            dma((kv_heads, REACH)),
            dma((kv_heads, REACH)),
            dma((ep_size - 1,)),
            dma((ep_size - 1,)),
            dma((seq_size - 1,)),
            dma((seq_size - 1,)),
            dma((ep_size - 1,)),
            dma((ep_size - 1,)),
        ],
        compiler_params=pltpu.CompilerParams(
            vmem_limit_bytes=VMEM_LIMIT, collective_id=0, has_side_effects=True
        ),
        cost_estimate=pl.CostEstimate(
            flops=work * HD * 10, bytes_accessed=tok * width * 6, transcendentals=work
        ),
        name="attention",
    )(start, segments, queries, attn_grad, key_heads, value_heads, part)


def split3(x):
    high = x.astype(BF16)
    rest = x - high.astype(F32)
    mid = rest.astype(BF16)
    low = (rest - mid.astype(F32)).astype(BF16)
    return jnp.concatenate([high.astype(F32), mid.astype(F32), low.astype(F32)], axis=0).astype(BF16)


def route_kernel(capacity, copies, all_tokens, routes_ref, moe_ref, expert_ref, normed_ref, router_ref,
                 ngrad_ref, rgrad_ref, out_ref):
    rows, width = moe_ref.shape
    slots = out_ref.shape[0]
    logits = nt(router_ref[...], normed_ref[...])
    expert = lax.broadcasted_iota(jnp.int32, (EXPERTS, rows), 0)
    e0 = routes_ref[0:1, :]
    e1 = routes_ref[1:2, :]
    hot0 = (expert == e0).astype(F32)
    hot1 = (expert == e1).astype(F32)
    chosen0 = jnp.sum(hot0 * logits, axis=0, keepdims=True)
    chosen1 = jnp.sum(hot1 * logits, axis=0, keepdims=True)
    first = 1.0 / (1.0 + jnp.exp(chosen1 - chosen0))
    second = 1.0 - first
    product = nt(expert_ref[...], moe_ref[...])
    which = lax.broadcasted_iota(jnp.int32, product.shape, 0)
    token = lax.broadcasted_iota(jnp.int32, product.shape, 1)
    signed = jnp.where(which == 2 * token, product, jnp.where(which == 2 * token + 1, -product, 0.0))
    step = first * second * jnp.sum(signed, axis=0, keepdims=True)
    pieces = split3((hot0 - hot1) * step)
    earlier = lax.broadcasted_iota(jnp.int32, (rows, rows), 0) < lax.broadcasted_iota(jnp.int32, (rows, rows), 1)
    rank = nn((hot0 + hot1).astype(BF16), earlier.astype(BF16))
    rank0 = jnp.sum(hot0 * rank, axis=0, keepdims=True).astype(jnp.int32)
    rank1 = jnp.sum(hot1 * rank, axis=0, keepdims=True).astype(jnp.int32)
    slot = lax.broadcasted_iota(jnp.int32, (slots, rows), 0)
    slot = (slot // (copies * capacity)) * capacity + slot % capacity
    take0 = slot == e0 * capacity + rank0
    take1 = slot == e1 * capacity + rank1
    gate = jnp.sum(jnp.where(take0, first, 0.0) + jnp.where(take1, second, 0.0), axis=1, keepdims=True)
    pick = (take0 | take1).astype(BF16)
    chunk = 512
    for at in range(0, width, chunk):
        columns = slice(at, at + chunk)
        out_ref[:, columns] = (nn(pick, moe_ref[:, columns]) * gate).astype(BF16)
        table = jnp.concatenate([router_ref[:, columns].astype(F32)] * 3, axis=0).astype(BF16)
        ngrad_ref[:, columns] = lax.dot_general(
            pieces, table, (((0,), (0,)), ((), ())), preferred_element_type=F32
        ).astype(BF16)
        sums = nn(pieces, normed_ref[:, columns])
        rgrad_ref[:, columns] = (
            sums[0:EXPERTS] + sums[EXPERTS:2 * EXPERTS] + sums[2 * EXPERTS:]
        ) * (1.0 / all_tokens)


def on_device(queries, key_heads, value_heads, attn_grad, segments, moe_grad, expert_out, normed, router, routes):
    tok = queries.shape[0]
    ep_size = lax.axis_size("ep")
    inside = jnp.sum((segments[:, None] < segments[None, :]).astype(jnp.int32), axis=0)
    start = (REACH * tok + inside)[None, :]

    moe_rows, width = moe_grad.shape
    capacity = moe_rows * TOP // EXPERTS
    copies = max(1, ep_size // EXPERTS)
    per_device = max(1, EXPERTS // ep_size)
    slots = EXPERTS * copies * capacity
    devices = lax.axis_size("seq") * ep_size
    normed_grad, local_router, outgoing = pl.pallas_call(
        functools.partial(route_kernel, capacity, copies, moe_rows * devices),
        out_shape=(
            jax.ShapeDtypeStruct((moe_rows, width), BF16),
            jax.ShapeDtypeStruct((EXPERTS, width), F32),
            jax.ShapeDtypeStruct((slots, width), BF16),
        ),
        compiler_params=pltpu.CompilerParams(vmem_limit_bytes=VMEM_LIMIT),
        cost_estimate=pl.CostEstimate(flops=8 * slots * moe_rows * width, bytes_accessed=12 * moe_rows * width, transcendentals=0),
        name="routing",
    )(routes.T, moe_grad, expert_out.reshape(TOP * moe_rows, width), normed, router)
    routed_grads = lax.all_to_all(
        outgoing.reshape(ep_size, per_device * capacity, width), "ep", split_axis=0, concat_axis=0, tiled=True
    )
    query_grad, key_grad, value_grad, router_grad = attention(
        start, jnp.broadcast_to(segments[None, :], (8, tok)), queries, attn_grad, key_heads, value_heads, local_router
    )
    return (query_grad, key_grad, value_grad, normed_grad, router_grad, routed_grads)


def solution(mesh):
    return jax.shard_map(
        on_device,
        mesh=mesh,
        in_specs=(
            P("seq", "ep"),
            P("seq", "ep"),
            P("seq", "ep"),
            P("seq", "ep"),
            P("seq"),
            P(("seq", "ep"), None),
            P(("seq", "ep"), None, None),
            P(("seq", "ep"), None),
            P(),
            P(("seq", "ep"), None),
        ),
        out_specs=(
            P("seq", "ep"),
            P("seq", "ep"),
            P("seq", "ep"),
            P(("seq", "ep"), None),
            P(),
            P(("seq", "ep"), None, None),
        ),
        check_vma=False,
    )
```

time: 140 us -> 111 us (0.79)
  the two profiles are of different devices: /device:TPU:10 before, /device:TPU:6 now
where the time goes in v1:
time: 111 us
  Pallas kernels  92.9 us (84%)
  local copies, waits for them, and re-layouts  12 us (11%)
  starting transfers between devices  5.13 us (5%)
    pallas_call x1, Pallas kernels, attention(): pl.pallas_call(functools.partial(attn_kernel, group, tok, kv_heads), in_s...  86.6 us
    unnamed x23, local copies, waits for them, and re-layouts  7.64 us
    pallas_call x1, Pallas kernels, on_device(): pl.pallas_call(functools.partial(route_kernel, capacity, copies, moe_rows...  6.28 us
    all_to_all x1, starting transfers between devices, on_device(): lax.all_to_all(outgoing.reshape(ep_size, per_device * capacity, width), '...  5.13 us
    reshape x1, local copies, waits for them, and re-layouts, on_device(): expert_out.reshape(TOP * moe_rows, width)  4.4 us
  transfers between devices with their start and end apart: 1, of which 0 were waited for; matrix products, arithmetic and copies ran while one was open for 0% of the time, Pallas kernels for 78%

profile of v1, /device:TPU:6, one launch (start us, length us, event | category | flops | bytes accessed | tf_op | source)
XLA Modules:
  0.0 111.0 jit_solution(14134361854606198238)
XLA Ops:
  0.6 0.0 copy-start.3
  0.6 0.0 copy-start.2
  0.7 0.0 copy-start.1
  0.7 0.0 copy-start
  0.7 4.4 %reshape.29.expert_ref = bf16[192,6144]{1,0:T(8,128)(2,1)} reshape(bf16[96,2,6144]{2,1,0:T(2,128)(2,1)} %param.16) | data formatting | bytes 4718592 | tf_op jit(solution)/shard_map/reshape | solution.py:333
  5.1 0.0 copy-done.3
  5.1 0.0 copy-done.2
  5.1 0.0 copy-done.1
  5.1 0.0 copy-done
  5.1 6.3 %routing.1 = (bf16[96,6144]{1,0:T(8,128)(2,1)}, f32[8,6144]{1,0:T(8,128)S(1)}, bf16[192,6144]{1,0:T(8,128)(2,1)}) custom-call(s32[2,96]{1,0:T(2,128)S(1)} %bitcast.2, bf16[96,6144]{1,0:T(8,128)(2,1)S(1)} %copy-done, bf16[192,6144]{1,0:T(8,128)(2,1)} %reshape.29.expert_ref, bf16[96,6144]{1,0:T(8,128)(2,1)S(1)} %copy-done.1, bf16[8,6144]{1,0:T(8,128)(2,1)S(1)} %copy-done.2), custom_call_target="tpu_custom_call" | custom-call | flops 905969664 | bytes 7077888 | tf_op jit(solution)/shard_map/routing/pallas_call | solution.py:323
  11.4 0.0 copy-start.8
  11.4 0.0 copy-start.4
  11.4 0.0 copy-start.6
  11.4 0.0 copy-start.7
  11.4 5.1 %all-to-all-start = ((bf16[4,48,6144]{2,1,0:T(8,128)(2,1)}), bf16[4,48,6144]{2,1,0:T(8,128)(2,1)}, u32[]{:S(2)}, u32[]{:S(2)}) async-start(bf16[4,48,6144]{2,1,0:T(8,128)(2,1)} %bitcast.1), calls=%async_computation | async-start | bytes 4718592 | tf_op jit(solution)/shard_map/all_to_all | solution.py:334
  16.5 0.0 copy-done.8
  16.5 0.1 convert_reduce_fusion
  16.7 0.0 copy-done.4
  16.7 0.0 copy-done.6
  16.7 0.0 copy-done.7
  16.7 0.0 copy-start.5
  16.7 1.3 %copy-done.5 = bf16[384,1536]{1,0:T(8,128)(2,1)S(1)} copy-done((bf16[384,1536]{1,0:T(8,128)(2,1)S(1)}, bf16[384,1536]{1,0:T(8,128)(2,1)}, u32[]{:S(2)}) %copy-start.5) | copy-done | bytes 1179672
  18.0 86.6 %attention.1 = (bf16[384,1536]{1,0:T(8,128)(2,1)S(1)}, bf16[384,256]{1,0:T(8,128)(2,1)S(1)}, bf16[384,256]{1,0:T(8,128)(2,1)S(1)}, f32[8,6144]{1,0:T(8,128)S(1)}) custom-call(s32[1,384]{1,0:T(1,128)S(1)} %add.18.start_in, s32[8,384]{1,0:T(8,128)S(1)} %broadcast_in_dim.2.seg_ref, bf16[384,1536]{1,0:T(8,128)(2,1)S(1)} %copy-done.4, ...), custom_call_target="tpu_custom_call" | custom-call | flops 7549747200 | bytes 14155776 | tf_op jit(solution)/shard_map/attention/pallas_call | solution.py:209
  104.6 0.0 all-to-all-done
  104.7 1.0 copy.21
  105.7 0.7 copy.22
  106.3 0.7 copy.23
  107.0 0.7 copy.24
  107.7 3.3 %copy.25 = bf16[4,48,6144]{2,1,0:T(8,128)(2,1)} copy(bf16[4,48,6144]{2,1,0:T(8,128)(2,1)} %all-to-all-done) | data formatting | bytes 4718592
  (3 shorter events, 0.0 us)
Async XLA Ops:
  0.6 4.4 %copy-start.3 = (s32[96,2]{0,1:T(2,128)S(1)}, s32[96,2]{0,1:T(2,128)}, u32[]{:S(2)}) copy-start(s32[96,2]{0,1:T(2,128)} %param.19) | copy-start | bytes 2308
  0.6 4.4 %copy-start.2 = (bf16[8,6144]{1,0:T(8,128)(2,1)S(1)}, bf16[8,6144]{1,0:T(8,128)(2,1)}, u32[]{:S(2)}) copy-start(bf16[8,6144]{1,0:T(8,128)(2,1)} %router_ref.1) | copy-start | bytes 294916
  0.7 4.4 %copy-start.1 = (bf16[96,6144]{1,0:T(8,128)(2,1)S(1)}, bf16[96,6144]{1,0:T(8,128)(2,1)}, u32[]{:S(2)}) copy-start(bf16[96,6144]{1,0:T(8,128)(2,1)} %normed_ref.1) | copy-start | bytes 3538948
  0.7 4.4 %copy-start = (bf16[96,6144]{1,0:T(8,128)(2,1)S(1)}, bf16[96,6144]{1,0:T(8,128)(2,1)}, u32[]{:S(2)}) copy-start(bf16[96,6144]{1,0:T(8,128)(2,1)} %moe_ref.1) | copy-start | bytes 3538948
  11.4 5.1 %copy-start.8 = (s32[384]{0:T(512)S(1)}, s32[384]{0:T(512)}, u32[]{:S(2)}) copy-start(s32[384]{0:T(512)} %param.14) | copy-start | bytes 4612
  11.4 5.3 %copy-start.4 = (bf16[384,1536]{1,0:T(8,128)(2,1)S(1)}, bf16[384,1536]{1,0:T(8,128)(2,1)}, u32[]{:S(2)}) copy-start(bf16[384,1536]{1,0:T(8,128)(2,1)} %q_ref.1) | copy-start | bytes 3538948
  11.4 5.3 %copy-start.6 = (bf16[384,256]{1,0:T(8,128)(2,1)S(1)}, bf16[384,256]{1,0:T(8,128)(2,1)}, u32[]{:S(2)}) copy-start(bf16[384,256]{1,0:T(8,128)(2,1)} %k_ref.1) | copy-start | bytes 589828
  11.4 5.3 %copy-start.7 = (bf16[384,256]{1,0:T(8,128)(2,1)S(1)}, bf16[384,256]{1,0:T(8,128)(2,1)}, u32[]{:S(2)}) copy-start(bf16[384,256]{1,0:T(8,128)(2,1)} %v_ref.1) | copy-start | bytes 589828
  11.4 93.2 %all-to-all-start = ((bf16[4,48,6144]{2,1,0:T(8,128)(2,1)}), bf16[4,48,6144]{2,1,0:T(8,128)(2,1)}, u32[]{:S(2)}, u32[]{:S(2)}) async-start(bf16[4,48,6144]{2,1,0:T(8,128)(2,1)} %bitcast.1), calls=%async_computation | async-start | bytes 4718592 | tf_op jit(solution)/shard_map/all_to_all | solution.py:334
  16.7 1.3 %copy-start.5 = (bf16[384,1536]{1,0:T(8,128)(2,1)S(1)}, bf16[384,1536]{1,0:T(8,128)(2,1)}, u32[]{:S(2)}) copy-start(bf16[384,1536]{1,0:T(8,128)(2,1)} %g_ref.1) | copy-start | bytes 3538948

commit v2 on v1

--- a/solution.py
+++ b/solution.py
@@ -64,29 +64,117 @@
     for n in range(REACH):
         seg_copies.append(send(seg_ref, segs.at[n], seg_send.at[n], seg_recv.at[n], seq_at(n + 1)))
         seg_copies[-1].start()
-    kv_copies = []
+    odd = lax.rem(seq_me, 2)
+    even_here = odd == 0
+    odd_here = odd == 1
+
+    def kv(h, kind):
+        columns = pl.ds(h * HD, HD)
+        second = pl.ds(tok, tok)
+        third = pl.ds(2 * tok, tok)
+        copies = []
+        for which, (source, buffer) in enumerate(((k_ref, kcat), (v_ref, vcat))):
+            if kind == 0:
+                src, rows, device = source.at[:, columns], second, seq_at(2)
+            elif kind == 1:
+                rows = pl.ds(pl.multiple_of(2 * odd * tok, QT), tok)
+                src, device = buffer.at[h, second, :], seq_at(1 - 2 * odd)
+            elif kind == 2:
+                src, rows, device = source.at[:, columns], third, seq_at(1)
+            else:
+                src, rows, device = buffer.at[h, third, :], pl.ds(0, tok), seq_at(2)
+            copies.append(send(
+                src, buffer.at[h, rows, :], kv_send.at[h, kind, which], kv_recv.at[h, kind, which], device
+            ))
+        return copies
+
+    def begin(copies):
+        for copy in copies:
+            copy.start()
+
+    def landed(copies):
+        for copy in copies:
+            copy.wait_recv()
+
+    def pass_pair(h):
+        landed(kv(h, 0))
+        begin(kv(h, 1))
+
+    def pass_on(h):
+        @pl.when(even_here)
+        def _():
+            landed(kv(h, 1))
+            begin(kv(h, 3))
+
+    def keys_here(h):
+        @pl.when(even_here)
+        def _():
+            landed(kv(h, 3))
+
+        @pl.when(odd_here)
+        def _():
+            landed(kv(h, 1))
+            landed(kv(h, 2))
+
+    def term(h, kind):
+        source = (2, 2, 0, 0, 1)[kind]
+        device = seq_at((-2, -1, -1, 1, -2)[kind])
+        return send(far.at[h, source], back.at[h, kind], far_send.at[h, kind], far_recv.at[h, kind], device)
+
+    def add_to(h, source, kind):
+        term(h, kind).wait_recv()
+        far[h, source] = (far[h, source].astype(F32) + back[h, kind].astype(F32)).astype(BF16)
+
+    def terms_out(h):
+        @pl.when(even_here)
+        def _():
+            term(h, 0).start()
+
+        @pl.when(odd_here)
+        def _():
+            term(h, 1).start()
+            term(h, 2).start()
+
+    def terms_even(h):
+        @pl.when(even_here)
+        def _():
+            add_to(h, 0, 0)
+            term(h, 3).start()
+            add_to(h, 1, 1)
+            term(h, 4).start()
+
+    def terms_odd(h):
+        @pl.when(odd_here)
+        def _():
+            add_to(h, 1, 3)
+            term(h, 4).start()
+
+    def terms_in(h):
+        @pl.when(even_here)
+        def _():
+            term(h, 2).wait_recv()
+            own[h] += back[h, 2].astype(F32)
+
+        term(h, 4).wait_recv()
+        terms = own[h] + back[h, 4].astype(F32)
+        dk_ref[:, h * HD:(h + 1) * HD] = terms[:, :HD].astype(BF16)
+        dv_ref[:, h * HD:(h + 1) * HD] = terms[:, HD:].astype(BF16)
+
+    one_copies = []
     for h in range(kv_heads):
-        for n in range(REACH):
-            rows = pl.ds((REACH - 1 - n) * tok, tok)
-            columns = pl.ds(h * HD, HD)
-            for which, (src, dst) in enumerate(((k_ref, kcat), (v_ref, vcat))):
-                kv_copies.append(send(
-                    src.at[:, columns], dst.at[h, rows, :],
-                    kv_send.at[h, n, which], kv_recv.at[h, n, which], seq_at(n + 1),
-                ))
+        begin(kv(h, 0))
+
+        @pl.when(even_here)
+        def _(h=h):
+            begin(kv(h, 2))
+
         if h == 0:
-            for copy in kv_copies:
-                copy.start()
-            one_copies = []
             for by in range(1, ep_size):
                 columns = pl.ds(pl.multiple_of(lax.rem(ep_me + by, ep_size) * chunk, 128), chunk)
                 one_copies.append(send(
                     part_ref.at[:, columns], one.at[by - 1], one_send.at[by - 1], one_recv.at[by - 1], ep_at(by)
                 ))
-                one_copies[-1].start()
-        else:
-            for copy in kv_copies[-2 * REACH:]:
-                copy.start()
+            begin(one_copies)
     for h in range(kv_heads):
         kcat[h, REACH * tok:, :] = k_ref[:, h * HD:(h + 1) * HD]
         vcat[h, REACH * tok:, :] = v_ref[:, h * HD:(h + 1) * HD]
@@ -119,10 +207,12 @@
 
     together = 2 if group % 2 == 0 else 1
     three_copies = []
-    far_copies = []
+    pass_pair(0)
+    pass_on(0)
+    for h in range(1, kv_heads):
+        pass_pair(h)
     for h in range(kv_heads):
-        for copy in kv_copies[2 * REACH * h:2 * REACH * (h + 1)]:
-            copy.wait_recv()
+        keys_here(h)
         for n in range(REACH + 1):
             rows = slice(n * tok, (n + 1) * tok)
             kt[:, rows] = kcat[h, rows, :].astype(F32).T.astype(BF16)
@@ -154,6 +244,19 @@
                 dq = (nn(kt[:, keys], score_low) * SCALE).T.astype(BF16)
                 for n, i in enumerate(heads):
                     dq_ref[rows, i * HD:(i + 1) * HD] = dq[n * QT:(n + 1) * QT, :]
+
+            @pl.when(step == 0)
+            def _():
+                if h + 1 < kv_heads:
+                    pass_on(h + 1)
+                if h > 0:
+                    terms_even(h - 1)
+
+            if h > 0:
+                @pl.when(step == 1)
+                def _():
+                    terms_odd(h - 1)
+
             return carry
 
         lax.fori_loop(0, tok // QT, rows_step, 0)
@@ -161,9 +264,7 @@
             rows = slice((REACH - 1 - n) * tok, (REACH - n) * tok)
             far[h, n, :, :HD] = (dk[rows, :] * SCALE).astype(BF16)
             far[h, n, :, HD:] = dv[rows, :].astype(BF16)
-            copy = send(far.at[h, n], back.at[h, n], far_send.at[h, n], far_recv.at[h, n], seq_at(-(n + 1)))
-            copy.start()
-            far_copies.append(copy)
+        terms_out(h)
         own[h, :, :HD] = dk[REACH * tok:, :] * SCALE
         own[h, :, HD:] = dv[REACH * tok:, :]
         if h == 0:
@@ -180,18 +281,29 @@
                 ))
                 three_copies[-1].start()
 
-    for copy in three_copies:
-        copy.wait_recv()
+    for h in range(kv_heads - 1):
+        terms_in(h)
+    terms_even(kv_heads - 1)
+    landed(three_copies)
     total_ref[...] = three[...]
+    terms_odd(kv_heads - 1)
+    terms_in(kv_heads - 1)
+
+    for copy in seg_copies + one_copies + two_copies + three_copies:
+        copy.wait_send()
     for h in range(kv_heads):
-        terms = own[h]
-        for n in range(REACH):
-            far_copies[h * REACH + n].wait_recv()
-            terms += back[h, n].astype(F32)
-        dk_ref[:, h * HD:(h + 1) * HD] = terms[:, :HD].astype(BF16)
-        dv_ref[:, h * HD:(h + 1) * HD] = terms[:, HD:].astype(BF16)
-    for copy in seg_copies + kv_copies + one_copies + two_copies + three_copies + far_copies:
-        copy.wait_send()
+        for copy in kv(h, 0) + kv(h, 1) + [term(h, 4)]:
+            copy.wait_send()
+
+        @pl.when(even_here)
+        def _(h=h):
+            for copy in kv(h, 2) + kv(h, 3) + [term(h, 0), term(h, 3)]:
+                copy.wait_send()
+
+        @pl.when(odd_here)
+        def _(h=h):
+            term(h, 1).wait_send()
+            term(h, 2).wait_send()
 
 
 def attention(start, segments, queries, attn_grad, key_heads, value_heads, part):
@@ -226,7 +338,7 @@
             pltpu.VMEM((1, tok), jnp.int32),
             pltpu.VMEM((kv_heads, tok, 2 * HD), F32),
             pltpu.VMEM((kv_heads, REACH, tok, 2 * HD), BF16),
-            pltpu.VMEM((kv_heads, REACH, tok, 2 * HD), BF16),
+            pltpu.VMEM((kv_heads, 5, tok, 2 * HD), BF16),
             pltpu.VMEM((REACH, 8, tok), jnp.int32),
             pltpu.VMEM((ep_size - 1, EXPERTS, chunk), F32),
             pltpu.VMEM((seq_size, EXPERTS, chunk), F32),
@@ -235,10 +347,10 @@
             pltpu.VMEM((EXPERTS, chunk), F32),
             dma((REACH,)),
             dma((REACH,)),
-            dma((kv_heads, REACH, 2)),
-            dma((kv_heads, REACH, 2)),
-            dma((kv_heads, REACH)),
-            dma((kv_heads, REACH)),
+            dma((kv_heads, 4, 2)),
+            dma((kv_heads, 4, 2)),
+            dma((kv_heads, 5)),
+            dma((kv_heads, 5)),
             dma((ep_size - 1,)),
             dma((ep_size - 1,)),
             dma((seq_size - 1,)),

time: 111 us -> 115 us (1.036)
  the two profiles are of different devices: /device:TPU:6 before, /device:TPU:20 now
where the time goes in v2:
time: 115 us; the launch traced here: 114 us
  Pallas kernels  96.5 us (84%)
  local copies, waits for them, and re-layouts  12 us (10%)
  starting transfers between devices  4.81 us (4%)
    pallas_call x1, Pallas kernels, attention(): pl.pallas_call(functools.partial(attn_kernel, group, tok, kv_heads), in_s...  90.2 us
    unnamed x23, local copies, waits for them, and re-layouts  7.64 us
    pallas_call x1, Pallas kernels, on_device(): pl.pallas_call(functools.partial(route_kernel, capacity, copies, moe_rows...  6.28 us
    all_to_all x1, starting transfers between devices, on_device(): lax.all_to_all(outgoing.reshape(ep_size, per_device * capacity, width), '...  4.81 us
    reshape x1, local copies, waits for them, and re-layouts, on_device(): expert_out.reshape(TOP * moe_rows, width)  4.4 us
  transfers between devices with their start and end apart: 1, of which 0 were waited for; matrix products, arithmetic and copies ran while one was open for 0% of the time, Pallas kernels for 79%

profile of v2, /device:TPU:20, one launch (start us, length us, event | category | flops | bytes accessed | tf_op | source)
XLA Modules:
  0.0 114.3 jit_solution(1700315306528789825)
XLA Ops:
  0.6 0.0 copy-start.3
  0.6 0.0 copy-start.2
  0.7 0.0 copy-start.1
  0.7 0.0 copy-start
  0.7 4.4 %reshape.29.expert_ref = bf16[192,6144]{1,0:T(8,128)(2,1)} reshape(bf16[96,2,6144]{2,1,0:T(2,128)(2,1)} %param.16) | data formatting | bytes 4718592 | tf_op jit(solution)/shard_map/reshape | solution.py:445
  5.1 0.0 copy-done.3
  5.1 0.0 copy-done.2
  5.1 0.0 copy-done.1
  5.1 0.0 copy-done
  5.1 6.3 %routing.1 = (bf16[96,6144]{1,0:T(8,128)(2,1)}, f32[8,6144]{1,0:T(8,128)S(1)}, bf16[192,6144]{1,0:T(8,128)(2,1)}) custom-call(s32[2,96]{1,0:T(2,128)S(1)} %bitcast.2, bf16[96,6144]{1,0:T(8,128)(2,1)S(1)} %copy-done, bf16[192,6144]{1,0:T(8,128)(2,1)} %reshape.29.expert_ref, bf16[96,6144]{1,0:T(8,128)(2,1)S(1)} %copy-done.1, bf16[8,6144]{1,0:T(8,128)(2,1)S(1)} %copy-done.2), custom_call_target="tpu_custom_call" | custom-call | flops 905969664 | bytes 7077888 | tf_op jit(solution)/shard_map/routing/pallas_call | solution.py:435
  11.4 0.0 copy-start.8
  11.4 0.0 copy-start.4
  11.4 0.0 copy-start.6
  11.4 0.0 copy-start.7
  11.4 4.8 %all-to-all-start = ((bf16[4,48,6144]{2,1,0:T(8,128)(2,1)}), bf16[4,48,6144]{2,1,0:T(8,128)(2,1)}, u32[]{:S(2)}, u32[]{:S(2)}) async-start(bf16[4,48,6144]{2,1,0:T(8,128)(2,1)} %bitcast.1), calls=%async_computation | async-start | bytes 4718592 | tf_op jit(solution)/shard_map/all_to_all | solution.py:446
  16.2 0.0 copy-done.8
  16.2 0.1 convert_reduce_fusion
  16.4 0.0 copy-done.4
  16.4 0.0 copy-done.6
  16.4 0.0 copy-done.7
  16.4 0.0 copy-start.5
  16.4 1.3 %copy-done.5 = bf16[384,1536]{1,0:T(8,128)(2,1)S(1)} copy-done((bf16[384,1536]{1,0:T(8,128)(2,1)S(1)}, bf16[384,1536]{1,0:T(8,128)(2,1)}, u32[]{:S(2)}) %copy-start.5) | copy-done | bytes 1179672
  17.7 90.2 %attention.1 = (bf16[384,1536]{1,0:T(8,128)(2,1)S(1)}, bf16[384,256]{1,0:T(8,128)(2,1)S(1)}, bf16[384,256]{1,0:T(8,128)(2,1)S(1)}, f32[8,6144]{1,0:T(8,128)S(1)}) custom-call(s32[1,384]{1,0:T(1,128)S(1)} %add.18.start_in, s32[8,384]{1,0:T(8,128)S(1)} %broadcast_in_dim.2.seg_ref, bf16[384,1536]{1,0:T(8,128)(2,1)S(1)} %copy-done.4, ...), custom_call_target="tpu_custom_call" | custom-call | flops 7549747200 | bytes 14155776 | tf_op jit(solution)/shard_map/attention/pallas_call | solution.py:321
  107.9 0.0 all-to-all-done
  107.9 1.0 copy.21
  108.9 0.7 copy.22
  109.6 0.7 copy.23
  110.3 0.7 copy.24
  111.0 3.3 %copy.25 = bf16[4,48,6144]{2,1,0:T(8,128)(2,1)} copy(bf16[4,48,6144]{2,1,0:T(8,128)(2,1)} %all-to-all-done) | data formatting | bytes 4718592
  (3 shorter events, 0.0 us)
Async XLA Ops:
  0.6 4.4 %copy-start.3 = (s32[96,2]{0,1:T(2,128)S(1)}, s32[96,2]{0,1:T(2,128)}, u32[]{:S(2)}) copy-start(s32[96,2]{0,1:T(2,128)} %param.19) | copy-start | bytes 2308
  0.6 4.4 %copy-start.2 = (bf16[8,6144]{1,0:T(8,128)(2,1)S(1)}, bf16[8,6144]{1,0:T(8,128)(2,1)}, u32[]{:S(2)}) copy-start(bf16[8,6144]{1,0:T(8,128)(2,1)} %router_ref.1) | copy-start | bytes 294916
  0.7 4.4 %copy-start.1 = (bf16[96,6144]{1,0:T(8,128)(2,1)S(1)}, bf16[96,6144]{1,0:T(8,128)(2,1)}, u32[]{:S(2)}) copy-start(bf16[96,6144]{1,0:T(8,128)(2,1)} %normed_ref.1) | copy-start | bytes 3538948
  0.7 4.4 %copy-start = (bf16[96,6144]{1,0:T(8,128)(2,1)S(1)}, bf16[96,6144]{1,0:T(8,128)(2,1)}, u32[]{:S(2)}) copy-start(bf16[96,6144]{1,0:T(8,128)(2,1)} %moe_ref.1) | copy-start | bytes 3538948
  11.4 4.8 %copy-start.8 = (s32[384]{0:T(512)S(1)}, s32[384]{0:T(512)}, u32[]{:S(2)}) copy-start(s32[384]{0:T(512)} %param.14) | copy-start | bytes 4612
  11.4 5.0 %copy-start.4 = (bf16[384,1536]{1,0:T(8,128)(2,1)S(1)}, bf16[384,1536]{1,0:T(8,128)(2,1)}, u32[]{:S(2)}) copy-start(bf16[384,1536]{1,0:T(8,128)(2,1)} %q_ref.1) | copy-start | bytes 3538948
  11.4 5.0 %copy-start.6 = (bf16[384,256]{1,0:T(8,128)(2,1)S(1)}, bf16[384,256]{1,0:T(8,128)(2,1)}, u32[]{:S(2)}) copy-start(bf16[384,256]{1,0:T(8,128)(2,1)} %k_ref.1) | copy-start | bytes 589828
  11.4 5.0 %copy-start.7 = (bf16[384,256]{1,0:T(8,128)(2,1)S(1)}, bf16[384,256]{1,0:T(8,128)(2,1)}, u32[]{:S(2)}) copy-start(bf16[384,256]{1,0:T(8,128)(2,1)} %v_ref.1) | copy-start | bytes 589828
  11.4 96.5 %all-to-all-start = ((bf16[4,48,6144]{2,1,0:T(8,128)(2,1)}), bf16[4,48,6144]{2,1,0:T(8,128)(2,1)}, u32[]{:S(2)}, u32[]{:S(2)}) async-start(bf16[4,48,6144]{2,1,0:T(8,128)(2,1)} %bitcast.1), calls=%async_computation | async-start | bytes 4718592 | tf_op jit(solution)/shard_map/all_to_all | solution.py:446
  16.4 1.3 %copy-start.5 = (bf16[384,1536]{1,0:T(8,128)(2,1)S(1)}, bf16[384,1536]{1,0:T(8,128)(2,1)}, u32[]{:S(2)}) copy-start(bf16[384,1536]{1,0:T(8,128)(2,1)} %g_ref.1) | copy-start | bytes 3538948

commit v3 on v2

--- a/solution.py
+++ b/solution.py
@@ -191,20 +191,6 @@
     start_ref[...] = start_in[...] - shift.astype(jnp.int32)
 
     mine = pl.ds(pl.multiple_of(ep_me * chunk, 128), chunk)
-    partial = part_ref[:, mine]
-    for copy in one_copies:
-        copy.wait_recv()
-    for by in range(1, ep_size):
-        partial += one[by - 1]
-    two_sum[...] = partial
-    two[seq_me] = partial
-    two_copies = []
-    for by in range(1, seq_size):
-        two_copies.append(send(
-            two_sum, two.at[seq_me], two_send.at[by - 1], two_recv.at[by - 1], seq_at(by)
-        ))
-        two_copies[-1].start()
-
     together = 2 if group % 2 == 0 else 1
     three_copies = []
     pass_pair(0)
@@ -268,25 +254,38 @@
         own[h, :, :HD] = dk[REACH * tok:, :] * SCALE
         own[h, :, HD:] = dv[REACH * tok:, :]
         if h == 0:
-            for copy in two_copies:
+            partial = part_ref[:, mine]
+            for copy in one_copies:
                 copy.wait_recv()
-            total = two[0]
-            for at in range(1, seq_size):
-                total += two[at]
-            three_sum[...] = total
-            three[:, mine] = total
             for by in range(1, ep_size):
-                three_copies.append(send(
-                    three_sum, three.at[:, mine], three_send.at[by - 1], three_recv.at[by - 1], ep_at(by)
+                partial += one[by - 1]
+            two_sum[...] = partial
+            two[seq_me] = partial
+            two_copies = []
+            for by in range(1, seq_size):
+                two_copies.append(send(
+                    two_sum, two.at[seq_me], two_send.at[by - 1], two_recv.at[by - 1], seq_at(by)
                 ))
-                three_copies[-1].start()
-
+                two_copies[-1].start()
+
+    for copy in two_copies:
+        copy.wait_recv()
+    total = two[0]
+    for at in range(1, seq_size):
+        total += two[at]
+    three_sum[...] = total
+    three[:, mine] = total
+    for by in range(1, ep_size):
+        three_copies.append(send(
+            three_sum, three.at[:, mine], three_send.at[by - 1], three_recv.at[by - 1], ep_at(by)
+        ))
+        three_copies[-1].start()
     for h in range(kv_heads - 1):
         terms_in(h)
     terms_even(kv_heads - 1)
+    terms_odd(kv_heads - 1)
     landed(three_copies)
     total_ref[...] = three[...]
-    terms_odd(kv_heads - 1)
     terms_in(kv_heads - 1)
 
     for copy in seg_copies + one_copies + two_copies + three_copies:

time: 115 us -> 93.4 us (0.81)
  Pallas kernels: 96.5 us -> 75.3 us
    pallas_call x1, Pallas kernels: 90.2 us -> 69 us  [attention(): pl.pallas_call(functools.partial(attn_kernel, group, tok, kv_heads), in_s...]
  transfers between devices with their start and end apart: 1 -> 1, of which waited for: 0 -> 0; matrix products, arithmetic and copies ran while one was open for 0% -> 0% of each run, Pallas kernels for 79% -> 74%
where the time goes in v3:
time: 93.4 us; the launch traced here: 93.1 us
  Pallas kernels  75.3 us (81%)
  local copies, waits for them, and re-layouts  12 us (13%)
  starting transfers between devices  4.81 us (5%)
    pallas_call x1, Pallas kernels, attention(): pl.pallas_call(functools.partial(attn_kernel, group, tok, kv_heads), in_s...  69 us
    unnamed x23, local copies, waits for them, and re-layouts  7.64 us
    pallas_call x1, Pallas kernels, on_device(): pl.pallas_call(functools.partial(route_kernel, capacity, copies, moe_rows...  6.28 us
    all_to_all x1, starting transfers between devices, on_device(): lax.all_to_all(outgoing.reshape(ep_size, per_device * capacity, width), '...  4.81 us
    reshape x1, local copies, waits for them, and re-layouts, on_device(): expert_out.reshape(TOP * moe_rows, width)  4.4 us
  transfers between devices with their start and end apart: 1, of which 0 were waited for; matrix products, arithmetic and copies ran while one was open for 0% of the time, Pallas kernels for 74%

profile of v3, /device:TPU:20, one launch (start us, length us, event | category | flops | bytes accessed | tf_op | source)
XLA Modules:
  0.0 93.1 jit_solution(4475134263069088274)
XLA Ops:
  0.6 0.0 copy-start.3
  0.6 0.0 copy-start.2
  0.7 0.0 copy-start.1
  0.7 0.0 copy-start
  0.7 4.4 %reshape.29.expert_ref = bf16[192,6144]{1,0:T(8,128)(2,1)} reshape(bf16[96,2,6144]{2,1,0:T(2,128)(2,1)} %param.16) | data formatting | bytes 4718592 | tf_op jit(solution)/shard_map/reshape | solution.py:444
  5.1 0.0 copy-done.3
  5.1 0.0 copy-done.2
  5.1 0.0 copy-done.1
  5.1 0.0 copy-done
  5.1 6.3 %routing.1 = (bf16[96,6144]{1,0:T(8,128)(2,1)}, f32[8,6144]{1,0:T(8,128)S(1)}, bf16[192,6144]{1,0:T(8,128)(2,1)}) custom-call(s32[2,96]{1,0:T(2,128)S(1)} %bitcast.2, bf16[96,6144]{1,0:T(8,128)(2,1)S(1)} %copy-done, bf16[192,6144]{1,0:T(8,128)(2,1)} %reshape.29.expert_ref, bf16[96,6144]{1,0:T(8,128)(2,1)S(1)} %copy-done.1, bf16[8,6144]{1,0:T(8,128)(2,1)S(1)} %copy-done.2), custom_call_target="tpu_custom_call" | custom-call | flops 905969664 | bytes 7077888 | tf_op jit(solution)/shard_map/routing/pallas_call | solution.py:434
  11.4 0.0 copy-start.8
  11.4 0.0 copy-start.4
  11.4 0.0 copy-start.6
  11.4 0.0 copy-start.7
  11.4 4.8 %all-to-all-start = ((bf16[4,48,6144]{2,1,0:T(8,128)(2,1)}), bf16[4,48,6144]{2,1,0:T(8,128)(2,1)}, u32[]{:S(2)}, u32[]{:S(2)}) async-start(bf16[4,48,6144]{2,1,0:T(8,128)(2,1)} %bitcast.1), calls=%async_computation | async-start | bytes 4718592 | tf_op jit(solution)/shard_map/all_to_all | solution.py:445
  16.2 0.0 copy-done.8
  16.2 0.1 convert_reduce_fusion
  16.4 0.0 copy-done.4
  16.4 0.0 copy-done.6
  16.4 0.0 copy-done.7
  16.4 0.0 copy-start.5
  16.4 1.3 %copy-done.5 = bf16[384,1536]{1,0:T(8,128)(2,1)S(1)} copy-done((bf16[384,1536]{1,0:T(8,128)(2,1)S(1)}, bf16[384,1536]{1,0:T(8,128)(2,1)}, u32[]{:S(2)}) %copy-start.5) | copy-done | bytes 1179672
  17.7 69.0 %attention.1 = (bf16[384,1536]{1,0:T(8,128)(2,1)S(1)}, bf16[384,256]{1,0:T(8,128)(2,1)S(1)}, bf16[384,256]{1,0:T(8,128)(2,1)S(1)}, f32[8,6144]{1,0:T(8,128)S(1)}) custom-call(s32[1,384]{1,0:T(1,128)S(1)} %add.18.start_in, s32[8,384]{1,0:T(8,128)S(1)} %broadcast_in_dim.2.seg_ref, bf16[384,1536]{1,0:T(8,128)(2,1)S(1)} %copy-done.4, ...), custom_call_target="tpu_custom_call" | custom-call | flops 7549747200 | bytes 14155776 | tf_op jit(solution)/shard_map/attention/pallas_call | solution.py:320
  86.7 0.0 all-to-all-done
  86.7 1.0 %copy.21 = bf16[384,1536]{1,0:T(8,128)(2,1)} copy(bf16[384,1536]{1,0:T(8,128)(2,1)S(1)} %get-tuple-element.26) | data formatting | bytes 2359296
  87.8 0.7 copy.22
  88.4 0.7 copy.23
  89.1 0.7 copy.24
  89.8 3.3 %copy.25 = bf16[4,48,6144]{2,1,0:T(8,128)(2,1)} copy(bf16[4,48,6144]{2,1,0:T(8,128)(2,1)} %all-to-all-done) | data formatting | bytes 4718592
  (3 shorter events, 0.0 us)
Async XLA Ops:
  0.6 4.4 %copy-start.3 = (s32[96,2]{0,1:T(2,128)S(1)}, s32[96,2]{0,1:T(2,128)}, u32[]{:S(2)}) copy-start(s32[96,2]{0,1:T(2,128)} %param.19) | copy-start | bytes 2308
  0.6 4.4 %copy-start.2 = (bf16[8,6144]{1,0:T(8,128)(2,1)S(1)}, bf16[8,6144]{1,0:T(8,128)(2,1)}, u32[]{:S(2)}) copy-start(bf16[8,6144]{1,0:T(8,128)(2,1)} %router_ref.1) | copy-start | bytes 294916
  0.7 4.4 %copy-start.1 = (bf16[96,6144]{1,0:T(8,128)(2,1)S(1)}, bf16[96,6144]{1,0:T(8,128)(2,1)}, u32[]{:S(2)}) copy-start(bf16[96,6144]{1,0:T(8,128)(2,1)} %normed_ref.1) | copy-start | bytes 3538948
  0.7 4.4 %copy-start = (bf16[96,6144]{1,0:T(8,128)(2,1)S(1)}, bf16[96,6144]{1,0:T(8,128)(2,1)}, u32[]{:S(2)}) copy-start(bf16[96,6144]{1,0:T(8,128)(2,1)} %moe_ref.1) | copy-start | bytes 3538948
  11.4 4.8 %copy-start.8 = (s32[384]{0:T(512)S(1)}, s32[384]{0:T(512)}, u32[]{:S(2)}) copy-start(s32[384]{0:T(512)} %param.14) | copy-start | bytes 4612
  11.4 5.0 %copy-start.4 = (bf16[384,1536]{1,0:T(8,128)(2,1)S(1)}, bf16[384,1536]{1,0:T(8,128)(2,1)}, u32[]{:S(2)}) copy-start(bf16[384,1536]{1,0:T(8,128)(2,1)} %q_ref.1) | copy-start | bytes 3538948
  11.4 5.0 %copy-start.6 = (bf16[384,256]{1,0:T(8,128)(2,1)S(1)}, bf16[384,256]{1,0:T(8,128)(2,1)}, u32[]{:S(2)}) copy-start(bf16[384,256]{1,0:T(8,128)(2,1)} %k_ref.1) | copy-start | bytes 589828
  11.4 5.0 %copy-start.7 = (bf16[384,256]{1,0:T(8,128)(2,1)S(1)}, bf16[384,256]{1,0:T(8,128)(2,1)}, u32[]{:S(2)}) copy-start(bf16[384,256]{1,0:T(8,128)(2,1)} %v_ref.1) | copy-start | bytes 589828
  11.4 75.3 %all-to-all-start = ((bf16[4,48,6144]{2,1,0:T(8,128)(2,1)}), bf16[4,48,6144]{2,1,0:T(8,128)(2,1)}, u32[]{:S(2)}, u32[]{:S(2)}) async-start(bf16[4,48,6144]{2,1,0:T(8,128)(2,1)} %bitcast.1), calls=%async_computation | async-start | bytes 4718592 | tf_op jit(solution)/shard_map/all_to_all | solution.py:445
  16.4 1.3 %copy-start.5 = (bf16[384,1536]{1,0:T(8,128)(2,1)S(1)}, bf16[384,1536]{1,0:T(8,128)(2,1)}, u32[]{:S(2)}) copy-start(bf16[384,1536]{1,0:T(8,128)(2,1)} %g_ref.1) | copy-start | bytes 3538948
